TPU v7x, 256 devices: a whole 4x4x8 slice. The times are simulated.
256 devices in a mesh: cuts: 16 (over y_hi, z), tile: 16 (over x, y_lo, core).
Axes of the slice: x: 4, y: 4 (y_hi: 2, y_lo: 2; y = y_hi * 2 + y_lo), z: 8, core: 2. Of those that a mesh axis runs over, the one named last changes fastest.
Arguments:
- field_in: float32 [384, 2, 256, 384], P('tile', None, 'cuts'), may hold values from -6 to 6
- propagator: bfloat16 [2, 384, 384], replicated
- theta: float32 [256, 32768], P('cuts', 'tile'), may hold values from -3.140625 to 3.140625
- cell_x: int32 [256, 2, 32768], P('cuts', None, 'tile'), may hold values from 0 to 23
- cell_y: int32 [256, 2, 32768], P('cuts', None, 'tile'), may hold values from 0 to 383
- src_dev: int32 [256, 2], replicated, may hold values from 0 to 15, all different within a row; in each aligned block of 16 rows (0 to 15, 16 to 31, ...) at most 4 rows name the same one
- src_slot: int32 [256, 2], replicated, may hold values from 0 to 15
- weights: float32 [256, 2], replicated, may hold values from 0.5 to 1.5
- coupling: float32 [2, 2], replicated, may hold values from 0.4 to 1.2
Outputs:
- field_out: float32 [384, 2, 256, 384], P('tile', None, 'cuts')
Inputs may be any that keep to these rules, and one draw needn't show every extreme that they name: `src_dev`: each row names 2 different values; in each aligned block of 16 rows no value is named by more than 4 rows.
All inputs are finite; a program needn't handle non-finite values.
Results may differ from a plain program's by a relative error of at most 0.0052.
Values may be sent and summed in bfloat16 or wider, within the bound.
A program may use at most 64 MiB of HBM per device.

v0:
```python
import functools
import math

import jax
import jax.numpy as jnp
from jax import lax
from jax.experimental import pallas as pl
from jax.experimental.pallas import tpu as pltpu
from jax.sharding import PartitionSpec as P

HARM = 5
CAP = 4
LANES = 128
MESH = pl.DeviceIdType.MESH
SIN_PI = (
    3.141592502593994,
    -5.1677069664001465,
    2.5500311851501465,
    -0.5980440974235535,
    0.07721816748380661,
)
F32 = jnp.float32
BF16 = jnp.bfloat16


def sin_pi(fraction):
    square = fraction * fraction
    total = jnp.full_like(square, SIN_PI[4])
    for coefficient in SIN_PI[3::-1]:
        total = total * square + coefficient
    return total * fraction


def dot_nn(left, right):
    return lax.dot_general(left, right, (((1,), (0,)), ((), ())), preferred_element_type=F32)


def dot_nt(left, right):
    return lax.dot_general(left, right, (((1,), (1,)), ((), ())), preferred_element_type=F32)


def rank_tables(me, dev, slot, cuts, tables):
    slices = dev.shape[1]
    per_block = slices // cuts
    source = lax.broadcasted_iota(jnp.int32, (cuts, slices), 0)
    low = lax.broadcasted_iota(jnp.int32, (slices, slices), 0)
    high = lax.broadcasted_iota(jnp.int32, (slices, slices), 1)
    same = low // per_block == high // per_block
    block = jnp.where(same, 1.0, 0.0).astype(BF16)
    before = jnp.where(same & (low < high), 1.0, 0.0).astype(BF16)
    hit0 = jnp.where(dev[0:1] == source, 1.0, 0.0)
    hit1 = jnp.where(dev[1:2] == source, 1.0, 0.0)
    rank0 = dot_nn(hit0.astype(BF16), before)
    rank1 = dot_nn(hit1.astype(BF16), before) + dot_nn(hit0.astype(BF16), block)
    rank0 = jnp.sum(hit0 * rank0, axis=0, keepdims=True)
    rank1 = jnp.sum(hit1 * rank1, axis=0, keepdims=True)
    arrival0 = dev[0:1] * CAP + rank0.astype(jnp.int32)
    arrival1 = dev[1:2] * CAP + rank1.astype(jnp.int32)
    tables[0:1, :] = arrival0
    tables[1:2, :] = arrival1
    wanted = lax.broadcasted_iota(jnp.int32, (8, slices), 0).astype(F32)
    mine0 = (dev[0:1] == me) & (rank0 == wanted)
    mine1 = (dev[1:2] == me) & (rank1 == wanted)
    slots = jnp.where(mine0, slot[0:1].astype(F32), 0.0) + jnp.where(mine1, slot[1:2].astype(F32), 0.0)
    place = lax.broadcasted_iota(jnp.int32, (slices, LANES), 0) // per_block
    column = lax.broadcasted_iota(jnp.int32, (slices, LANES), 1)
    chosen = dot_nn(slots.astype(BF16), jnp.where(place == column, 1.0, 0.0).astype(BF16))
    tables[8:16, 0:LANES] = chosen.astype(jnp.int32)


def section_kernel(
    cuts,
    tiles,
    theta_ref,
    dev_ref,
    slot_ref,
    weight_ref,
    coupling_ref,
    field_hbm,
    prop_hbm,
    cellx_hbm,
    celly_hbm,
    out_ref,
    field_v,
    prop_v,
    cellx_v,
    celly_v,
    tables_v,
    tables_s,
    phase_v,
    outgoing,
    arrived,
    row_code,
    col_code,
    full,
    round_send,
    source_send,
    hop,
    round_recv,
    source_recv,
    wide,
    tall,
    diff,
    back_send,
    back_recv,
    local_sem,
    theta_ss,
    theta_rs,
    round_ss,
    round_rs,
    source_ss,
    source_rs,
    hop_ss,
    hop_rs,
    back_ss,
    back_rs,
):
    c = lax.axis_index("cuts")
    t = lax.axis_index("tile")
    slots = theta_ref.shape[0]
    share = theta_ref.shape[1]
    pieces = share // LANES
    grid = prop_v.shape[1]
    rows = grid // tiles
    parts = 2 * rows

    barrier = pltpu.get_barrier_semaphore()

    def greet_cut(step, carry):
        pl.semaphore_signal(barrier, inc=1, device_id=(lax.rem(c + step, cuts), t), device_id_type=MESH)
        return carry

    def greet_tile(step, carry):
        pl.semaphore_signal(barrier, inc=1, device_id=(c, lax.rem(t + step, tiles)), device_id_type=MESH)
        return carry

    lax.fori_loop(1, cuts, greet_cut, 0)
    lax.fori_loop(1, tiles, greet_tile, 0)

    loads = [
        pltpu.make_async_copy(cellx_hbm, cellx_v, local_sem.at[0]),
        pltpu.make_async_copy(celly_hbm, celly_v, local_sem.at[1]),
        pltpu.make_async_copy(prop_hbm, prop_v, local_sem.at[2]),
    ] + [
        pltpu.make_async_copy(
            field_hbm.at[:, pl.ds(q * LANES, LANES)], field_v.at[q, pl.ds(0, 2 * slots * rows)], local_sem.at[3 + q]
        )
        for q in range(grid // LANES)
    ]
    for load in loads:
        load.start()

    rank_tables(c, dev_ref[...], slot_ref[...], cuts, tables_v)
    to_scalar = pltpu.make_async_copy(tables_v, tables_s, local_sem.at[6])
    to_scalar.start()

    turns = theta_ref[...] * (HARM / (2.0 * math.pi))
    turns = turns - jnp.floor(turns + 0.5)
    turns = jnp.minimum(jnp.floor(turns * 65536.0 + 0.5), 32767.0)
    for piece in range(pieces):
        phase_v[:, piece, :] = turns[:, piece * LANES : (piece + 1) * LANES]
    to_scalar.wait()

    def pick(block, carry):
        for rank in range(CAP):
            chosen = jnp.clip(tables_s[8 + rank, block], 0, slots - 1)
            outgoing[block * CAP + rank] = phase_v[chosen].astype(jnp.int32).astype(jnp.int16)
        return carry

    lax.fori_loop(0, cuts, pick, 0)
    pl.semaphore_wait(barrier, cuts + tiles - 2)

    def theta_copy(to, slot_of, sem_of):
        return pltpu.make_async_remote_copy(
            src_ref=outgoing.at[pl.ds(to * CAP, CAP)],
            dst_ref=arrived.at[pl.ds(slot_of * CAP, CAP)],
            send_sem=theta_ss.at[to],
            recv_sem=theta_rs.at[sem_of],
            device_id=(to, t),
            device_id_type=MESH,
        )

    def theta_start(step, carry):
        theta_copy(lax.rem(c + step, cuts), c, c).start()
        return carry

    lax.fori_loop(1, cuts, theta_start, 0)
    own_theta = pltpu.make_async_copy(
        outgoing.at[pl.ds(c * CAP, CAP)], arrived.at[pl.ds(c * CAP, CAP)], theta_rs.at[c]
    )
    own_theta.start()

    loads[0].wait()
    loads[1].wait()

    def codes(index, carry):
        cell_x = cellx_v[index]
        cell_y = celly_v[index]
        code = (cell_y // LANES) * rows + cell_x
        column = cell_y % LANES
        for k in range(2):
            row_code[2 * index + k] = jnp.broadcast_to(code[k : k + 1].astype(F32), (16, share)).astype(BF16)
            col_code[2 * index + k] = jnp.broadcast_to(column[k : k + 1].astype(F32), (16, share)).astype(BF16)
        return carry

    lax.fori_loop(0, slots, codes, 0)
    loads[2].wait()
    full[0:grid, 0:grid] = prop_v[0]
    full[0:grid, grid:] = -prop_v[1]
    full[grid:, 0:grid] = prop_v[1]
    full[grid:, grid:] = prop_v[0]
    for load in loads[3:]:
        load.wait()

    own_theta.wait()

    def theta_end(step, carry):
        other = lax.rem(c + step, cuts)
        theta_copy(other, other, other).wait_recv()
        return carry

    lax.fori_loop(1, cuts, theta_end, 0)

    width = 4 * LANES
    subs = lax.broadcasted_iota(jnp.int32, (16, width), 0)
    levels = [(subs + 16 * level).astype(F32).astype(BF16) for level in range(8)]
    one = jnp.ones((16, width), BF16)
    zero = jnp.zeros((16, width), BF16)
    c0r, c0i = coupling_ref[0, 0], coupling_ref[0, 1]
    c1r, c1i = coupling_ref[1, 0], coupling_ref[1, 1]

    def emit(slot):
        total = None
        for k in range(2):
            entry = c * slots + slot
            row = jnp.clip(tables_s[k, entry], 0, cuts * CAP - 1)
            weight = weight_ref[k, entry]
            phase = arrived[row].astype(jnp.int32).astype(F32) * (1.0 / 32768.0)
            cosine = sin_pi(0.5 - jnp.abs(phase))
            sine = sin_pi(jnp.maximum(jnp.minimum(phase, 1.0 - phase), -1.0 - phase))
            value_re = weight * cosine
            value_im = weight * sine
            index = 2 * slot + k
            for group in range(pieces // 4):
                lanes = slice(group * width, (group + 1) * width)
                column = col_code[index, :, lanes]
                code = row_code[index, :, lanes]
                spread_re = jnp.concatenate(
                    [jnp.broadcast_to(value_re[4 * group + i : 4 * group + i + 1], (16, LANES)) for i in range(4)], 1
                ).astype(BF16)
                spread_im = jnp.concatenate(
                    [jnp.broadcast_to(value_im[4 * group + i : 4 * group + i + 1], (16, LANES)) for i in range(4)], 1
                ).astype(BF16)
                hits = [code == level for level in levels[:5]]
                left = jnp.concatenate(
                    [jnp.where(hit, spread_re, zero) for hit in hits]
                    + [jnp.where(hit, spread_im, zero) for hit in hits],
                    0,
                )
                right = jnp.concatenate([jnp.where(column == level, one, zero) for level in levels], 0)
                product = dot_nt(left, right)
                total = product if total is None else total + product
        real_part = jnp.concatenate([total[i * rows : (i + 1) * rows] for i in range(3)], 1)
        imag_part = jnp.concatenate([total[80 + i * rows : 80 + (i + 1) * rows] for i in range(3)], 1)
        source = jnp.concatenate([real_part, imag_part], 0).astype(BF16)
        source_send[slot] = source
        source = source.astype(F32)
        real_part, imag_part = source[:rows], source[rows:]
        field_re = jnp.concatenate(
            [field_v[q, pl.ds(slot, rows, stride=2 * slots), :] for q in range(grid // LANES)], 1
        )
        field_im = jnp.concatenate(
            [field_v[q, pl.ds(slot + slots, rows, stride=2 * slots), :] for q in range(grid // LANES)], 1
        )
        sum_re = field_re + c0r * real_part - c0i * imag_part
        sum_im = field_im + c0r * imag_part + c0i * real_part
        round_send[slot] = jnp.concatenate([sum_re, sum_im], 0).astype(BF16)

    def hop_copy(which, src):
        return pltpu.make_async_remote_copy(
            src_ref=src,
            dst_ref=hop.at[which],
            send_sem=hop_ss.at[which],
            recv_sem=hop_rs.at[which],
            device_id=(lax.rem(c + 1, cuts), t),
            device_id_type=MESH,
        )

    def block_copy(src, dst, to, send, recv, sem_of):
        return pltpu.make_async_remote_copy(
            src_ref=src,
            dst_ref=dst,
            send_sem=send.at[to],
            recv_sem=recv.at[sem_of],
            device_id=(c, to),
            device_id_type=MESH,
        )

    def deliver(src, dst, to, send, recv):
        @pl.when(to == t)
        def _():
            pltpu.make_async_copy(src, dst.at[t], recv.at[t]).start()

        @pl.when(to != t)
        def _():
            block_copy(src, dst.at[t], to, send, recv, t).start()

    emit(slots - 1)
    hop_copy(1, round_send.at[slots - 1]).start()
    hop_copy(2, source_send.at[slots - 1]).start()
    emit(slots - 2)
    hop_copy(0, round_send.at[slots - 2]).start()
    deliver(source_send.at[slots - 2], source_recv, slots - 1, source_ss, source_rs)

    def forward():
        hop_copy(0, round_send.at[0]).wait_recv()
        deliver(hop.at[0], round_recv, 0, round_ss, round_rs)
        hop_copy(1, round_send.at[0]).wait_recv()
        deliver(hop.at[1], round_recv, 1, round_ss, round_rs)
        hop_copy(2, source_send.at[0]).wait_recv()
        deliver(hop.at[2], source_recv, 0, source_ss, source_rs)

    def one_slot(step, carry):
        slot = lax.rem(t + step, slots - 2)
        emit(slot)
        deliver(round_send.at[slot], round_recv, slot + 2, round_ss, round_rs)
        deliver(source_send.at[slot], source_recv, slot + 1, source_ss, source_rs)

        @pl.when(step == 5)
        def _():
            forward()

        return carry

    lax.fori_loop(0, slots - 2, one_slot, 0)

    def receive(src, dst, send, recv):
        pltpu.make_async_copy(src.at[0], dst.at[t], recv.at[t]).wait()

        def one(step, carry):
            other = lax.rem(t + step, tiles)
            block_copy(src.at[0], dst.at[other], other, send, recv, other).wait_recv()
            return carry

        lax.fori_loop(1, tiles, one, 0)

    receive(round_send, round_recv, round_ss, round_rs)

    def pair_of(ref, pair):
        first = ref[2 * pair].astype(F32)
        second = ref[2 * pair + 1].astype(F32)
        real_part = jnp.concatenate([first[:rows], second[:rows]], 0)
        imag_part = jnp.concatenate([first[rows:], second[rows:]], 0)
        return real_part, imag_part

    for pair in range(tiles // 2):
        real_part, imag_part = pair_of(round_recv, pair)
        wide[pair * parts : (pair + 1) * parts, 0:grid] = real_part.astype(BF16)
        wide[pair * parts : (pair + 1) * parts, grid:] = imag_part.astype(BF16)
    inter = dot_nt(wide[...], full[...])
    tall[0:grid, :] = inter[:, 0:grid].astype(BF16)
    tall[grid:, :] = inter[:, grid:].astype(BF16)
    diff[...] = dot_nn(full[...], tall[...])
    receive(source_send, source_recv, source_ss, source_rs)
    for pair in range(tiles // 2):
        real_part, imag_part = pair_of(source_recv, pair)
        top = slice(pair * parts, (pair + 1) * parts)
        low = slice(grid + pair * parts, grid + (pair + 1) * parts)
        tall[top, :] = (diff[top, :] + c1r * real_part - c1i * imag_part).astype(BF16)
        tall[low, :] = (diff[low, :] + c1r * imag_part + c1i * real_part).astype(BF16)

    def chunk_out(step, carry):
        chunk = lax.rem(t // 4 + step, tiles // 4)
        start = pl.multiple_of(chunk * 4 * rows, 4 * rows)
        inter_re = dot_nn(full[pl.ds(start, 4 * rows), :], tall[...])
        inter_im = dot_nn(full[pl.ds(start + grid, 4 * rows), :], tall[...])
        for i in range(4):
            to = 4 * chunk + i
            back_send[to] = jnp.concatenate(
                [inter_re[i * rows : (i + 1) * rows], inter_im[i * rows : (i + 1) * rows]], 0
            ).astype(BF16)
            deliver(back_send.at[to], back_recv, to, back_ss, back_rs)
        return carry

    lax.fori_loop(0, tiles // 4, chunk_out, 0)
    receive(back_send, back_recv, back_ss, back_rs)

    for slot in range(slots):
        block = back_recv[slot].astype(F32)
        for q in range(grid // LANES):
            lanes = slice(q * LANES, (q + 1) * LANES)
            field_v[q, pl.ds(slot, rows, stride=slots), :] = block[:rows, lanes]
            field_v[q, pl.ds(grid + slot, rows, stride=slots), :] = block[rows:, lanes]
    for q in range(grid // LANES):
        out_ref[:, q * LANES : (q + 1) * LANES] = field_v[q, 0:grid, :].astype(BF16)
        out_ref[:, grid + q * LANES : grid + (q + 1) * LANES] = field_v[q, grid : 2 * grid, :].astype(BF16)

    def sent_theta(step, carry):
        other = lax.rem(c + step, cuts)
        theta_copy(other, other, other).wait_send()
        return carry

    lax.fori_loop(1, cuts, sent_theta, 0)

    def sent(step, carry):
        other = lax.rem(t + step, tiles)
        block_copy(round_send.at[0], round_recv.at[0], other, round_ss, round_rs, other).wait_send()
        block_copy(source_send.at[0], source_recv.at[0], other, source_ss, source_rs, other).wait_send()
        block_copy(back_send.at[0], back_recv.at[0], other, back_ss, back_rs, other).wait_send()
        return carry

    lax.fori_loop(1, tiles, sent, 0)
    for which in range(3):
        hop_copy(which, round_send.at[0]).wait_send()


def final_kernel(wide_ref, prop_ref, out_ref):
    grid = prop_ref.shape[1]
    rows, _, slots, _ = out_ref.shape
    real_part = wide_ref[:, 0:grid]
    imag_part = wide_ref[:, grid:]
    out_re = dot_nt(real_part, prop_ref[0]) - dot_nt(imag_part, prop_ref[1])
    out_ref[:, 0] = out_re.reshape(rows, slots, grid)
    out_im = dot_nt(imag_part, prop_ref[0]) + dot_nt(real_part, prop_ref[1])
    out_ref[:, 1] = out_im.reshape(rows, slots, grid)


def on_device(cuts, tiles, field_in, propagator, theta, cell_x, cell_y, src_dev, src_slot, weights, coupling):
    grid = propagator.shape[1]
    rows = grid // tiles
    slots, share = theta.shape
    vmem = pl.BlockSpec(memory_space=pltpu.VMEM)
    smem = pl.BlockSpec(memory_space=pltpu.SMEM)
    anywhere = pl.BlockSpec(memory_space=pl.ANY)
    block = (2 * rows, grid)
    dma = pltpu.SemaphoreType.DMA
    wide = pl.pallas_call(
        functools.partial(section_kernel, cuts, tiles),
        out_shape=jax.ShapeDtypeStruct((grid, 2 * grid), BF16),
        in_specs=[vmem, vmem, vmem, smem, smem, anywhere, anywhere, anywhere, anywhere],
        out_specs=vmem,
        scratch_shapes=[
            pltpu.VMEM((grid // LANES, (rows + 1) * 2 * slots, LANES), F32),
            pltpu.VMEM((2, grid, grid), BF16),
            pltpu.VMEM((slots, 2, share), jnp.int32),
            pltpu.VMEM((slots, 2, share), jnp.int32),
            pltpu.VMEM((16, src_dev.shape[0]), jnp.int32),
            pltpu.SMEM((16, src_dev.shape[0]), jnp.int32),
            pltpu.VMEM((slots, share // LANES, LANES), F32),
            pltpu.VMEM((cuts * CAP, share // LANES, LANES), jnp.int16),
            pltpu.VMEM((cuts * CAP, share // LANES, LANES), jnp.int16),
            pltpu.VMEM((2 * slots, 16, share), BF16),
            pltpu.VMEM((2 * slots, 16, share), BF16),
            pltpu.VMEM((2 * grid, 2 * grid), BF16),
            pltpu.VMEM((slots,) + block, BF16),
            pltpu.VMEM((slots,) + block, BF16),
            pltpu.VMEM((3,) + block, BF16),
            pltpu.VMEM((tiles,) + block, BF16),
            pltpu.VMEM((tiles,) + block, BF16),
            pltpu.VMEM((grid, 2 * grid), BF16),
            pltpu.VMEM((2 * grid, grid), BF16),
            pltpu.VMEM((2 * grid, grid), F32),
            pltpu.VMEM((tiles,) + block, BF16),
            pltpu.VMEM((tiles,) + block, BF16),
            dma((7,)),
            dma((cuts,)),
            dma((cuts,)),
            dma((tiles,)),
            dma((tiles,)),
            dma((tiles,)),
            dma((tiles,)),
            dma((3,)),
            dma((3,)),
            dma((tiles,)),
            dma((tiles,)),
        ],
        compiler_params=pltpu.CompilerParams(
            collective_id=0, has_side_effects=True, vmem_limit_bytes=48 * 1024 * 1024
        ),
    )(
        theta,
        src_dev.T,
        src_slot.T,
        weights.T,
        coupling,
        field_in.reshape(rows * 2 * slots, grid),
        propagator,
        cell_x,
        cell_y,
    )
    return pl.pallas_call(
        final_kernel,
        out_shape=jax.ShapeDtypeStruct((rows, 2, slots, grid), F32),
        in_specs=[vmem, vmem],
        out_specs=vmem,
        compiler_params=pltpu.CompilerParams(vmem_limit_bytes=32 * 1024 * 1024),
    )(wide, propagator)


def solution(mesh):
    in_specs = (
        P("tile", None, "cuts", None),
        P(),
        P("cuts", "tile"),
        P("cuts", None, "tile"),
        P("cuts", None, "tile"),
        P(),
        P(),
        P(),
        P(),
    )
    out_specs = P("tile", None, "cuts", None)
    run = functools.partial(on_device, mesh.shape["cuts"], mesh.shape["tile"])
    return jax.shard_map(run, mesh=mesh, in_specs=in_specs, out_specs=out_specs, check_vma=False)
```

profile of v0, /device:TPU:1, one launch (start us, length us, event | category | flops | bytes accessed | tf_op | source)
XLA Modules:
  0.0 61.7 jit_solution(3612781374197603716)
XLA Ops:
  0.0 0.0 copy-start
  0.0 1.1 %copy-done = bf16[2,384,384]{2,1,0:T(8,128)(2,1)S(1)} copy-done((bf16[2,384,384]{2,1,0:T(8,128)(2,1)S(1)}, bf16[2,384,384]{2,1,0:T(8,128)(2,1)}, u32[]{:S(2)}) %copy-start) | copy-done | bytes 589848
  1.1 0.0 copy-start.1
  1.1 1.3 %copy-done.1 = f32[24,2,16,384]{3,2,1,0:T(8,128)S(1)} copy-done((f32[24,2,16,384]{3,2,1,0:T(8,128)S(1)}, f32[24,2,16,384]{3,2,1,0:T(8,128)}, u32[]{:S(2)}) %copy-start.1) | copy-done | bytes 1179672
  2.3 0.0 copy-start.2
  2.3 0.9 %copy-done.2 = s32[16,2,2048]{2,1,0:T(2,128)S(1)} copy-done((s32[16,2,2048]{2,1,0:T(2,128)S(1)}, s32[16,2,2048]{2,1,0:T(2,128)}, u32[]{:S(2)}) %copy-start.2) | copy-done | bytes 262168
  3.3 0.0 copy-start.3
  3.3 0.9 %copy-done.3 = s32[16,2,2048]{2,1,0:T(2,128)S(1)} copy-done((s32[16,2,2048]{2,1,0:T(2,128)S(1)}, s32[16,2,2048]{2,1,0:T(2,128)}, u32[]{:S(2)}) %copy-start.3) | copy-done | bytes 262168
  4.2 0.0 copy-start.4
  4.2 0.9 %copy-done.4 = f32[16,2048]{1,0:T(8,128)S(1)} copy-done((f32[16,2048]{1,0:T(8,128)S(1)}, f32[16,2048]{1,0:T(8,128)}, u32[]{:S(2)}) %copy-start.4) | copy-done | bytes 131096
  5.1 0.0 copy-start.5
  5.1 0.7 %copy-done.5 = s32[256,2]{0,1:T(2,128)S(1)} copy-done((s32[256,2]{0,1:T(2,128)S(1)}, s32[256,2]{0,1:T(2,128)}, u32[]{:S(2)}) %copy-start.5) | copy-done | bytes 2072
  5.8 0.0 copy-start.6
  5.8 0.7 %copy-done.6 = s32[256,2]{0,1:T(2,128)S(1)} copy-done((s32[256,2]{0,1:T(2,128)S(1)}, s32[256,2]{0,1:T(2,128)}, u32[]{:S(2)}) %copy-start.6) | copy-done | bytes 2072
  6.5 0.0 copy-start.7
  6.5 0.7 %copy-done.7 = f32[256,2]{0,1:T(2,128)S(1)} copy-done((f32[256,2]{0,1:T(2,128)S(1)}, f32[256,2]{0,1:T(2,128)}, u32[]{:S(2)}) %copy-start.7) | copy-done | bytes 2072
  7.2 0.0 copy-start.8
  7.2 0.7 %copy-done.8 = f32[2,2]{1,0:T(2,128)S(1)} copy-done((f32[2,2]{1,0:T(2,128)S(1)}, f32[2,2]{1,0:T(2,128)}, u32[]{:S(2)}) %copy-start.8) | copy-done | bytes 40
  7.9 52.0 %shard_map.91.wide_ref = bf16[384,768]{1,0:T(8,128)(2,1)S(1)} custom-call(f32[16,2048]{1,0:T(8,128)S(1)} %copy-done.4, s32[2,256]{1,0:T(2,128)S(1)} %bitcast.5, s32[2,256]{1,0:T(2,128)S(1)} %bitcast.6, f32[2,256]{1,0:T(2,128)S(1)} %bitcast.7, f32[2,2]{1,0:T(2,128)S(1)} %copy-done.8, f32[768,384]{1,0:T(8,128)S(1)} %bitcast.4, ...), custom_call_target="tpu_custom_call" | custom-call | tf_op jit(solution)/shard_map/pallas_call | solution.py:437
  59.8 1.9 %shard_map.92 = f32[24,2,16,384]{3,2,1,0:T(8,128)} custom-call(bf16[384,768]{1,0:T(8,128)(2,1)S(1)} %shard_map.91.wide_ref, bf16[2,384,384]{2,1,0:T(8,128)(2,1)S(1)} %copy-done), custom_call_target="tpu_custom_call" | custom-call | tf_op jit(solution)/shard_map/pallas_call | solution.py:491
Async XLA Ops:
  0.0 1.1 %copy-start = (bf16[2,384,384]{2,1,0:T(8,128)(2,1)S(1)}, bf16[2,384,384]{2,1,0:T(8,128)(2,1)}, u32[]{:S(2)}) copy-start(bf16[2,384,384]{2,1,0:T(8,128)(2,1)} %prop_ref.1) | copy-start | bytes 1769476
  1.1 1.3 %copy-start.1 = (f32[24,2,16,384]{3,2,1,0:T(8,128)S(1)}, f32[24,2,16,384]{3,2,1,0:T(8,128)}, u32[]{:S(2)}) copy-start(f32[24,2,16,384]{3,2,1,0:T(8,128)} %param.9) | copy-start | bytes 3538948
  2.3 0.9 %copy-start.2 = (s32[16,2,2048]{2,1,0:T(2,128)S(1)}, s32[16,2,2048]{2,1,0:T(2,128)}, u32[]{:S(2)}) copy-start(s32[16,2,2048]{2,1,0:T(2,128)} %cellx_hbm.1) | copy-start | bytes 786436
  3.3 0.9 %copy-start.3 = (s32[16,2,2048]{2,1,0:T(2,128)S(1)}, s32[16,2,2048]{2,1,0:T(2,128)}, u32[]{:S(2)}) copy-start(s32[16,2,2048]{2,1,0:T(2,128)} %celly_hbm.1) | copy-start | bytes 786436
  4.2 0.9 %copy-start.4 = (f32[16,2048]{1,0:T(8,128)S(1)}, f32[16,2048]{1,0:T(8,128)}, u32[]{:S(2)}) copy-start(f32[16,2048]{1,0:T(8,128)} %theta_ref.1) | copy-start | bytes 393220
  5.1 0.7 %copy-start.5 = (s32[256,2]{0,1:T(2,128)S(1)}, s32[256,2]{0,1:T(2,128)}, u32[]{:S(2)}) copy-start(s32[256,2]{0,1:T(2,128)} %param.14) | copy-start | bytes 6148
  5.8 0.7 %copy-start.6 = (s32[256,2]{0,1:T(2,128)S(1)}, s32[256,2]{0,1:T(2,128)}, u32[]{:S(2)}) copy-start(s32[256,2]{0,1:T(2,128)} %param.15) | copy-start | bytes 6148
  6.5 0.7 %copy-start.7 = (f32[256,2]{0,1:T(2,128)S(1)}, f32[256,2]{0,1:T(2,128)}, u32[]{:S(2)}) copy-start(f32[256,2]{0,1:T(2,128)} %param.16) | copy-start | bytes 6148
  7.2 0.7 %copy-start.8 = (f32[2,2]{1,0:T(2,128)S(1)}, f32[2,2]{1,0:T(2,128)}, u32[]{:S(2)}) copy-start(f32[2,2]{1,0:T(2,128)} %coupling_ref.1) | copy-start | bytes 52
where the time goes:
time: 62.1 us; the launch traced here: 61.7 us
  Pallas kernels  53.9 us (87%)
  local copies, waits for them, and re-layouts  7.86 us (13%)
    pallas_call x1, Pallas kernels, on_device(): pl.pallas_call(functools.partial(section_kernel, cuts, tiles), out_shape=...  52 us
    unnamed x18, local copies, waits for them, and re-layouts  7.86 us
    pallas_call x1, Pallas kernels, on_device(): pl.pallas_call(final_kernel, out_shape=jax.ShapeDtypeStruct((rows, 2, slo...  1.91 us

commit v1 on v0

v1 whole, which is shorter than its diff:
```python
import functools
import math

import jax
import jax.numpy as jnp
from jax import lax
from jax.experimental import pallas as pl
from jax.experimental.pallas import tpu as pltpu
from jax.sharding import PartitionSpec as P

HARM = 5
CAP = 4
LANES = 128
MESH = pl.DeviceIdType.MESH
SIN_PI = (
    3.141592502593994,
    -5.1677069664001465,
    2.5500311851501465,
    -0.5980440974235535,
    0.07721816748380661,
)
F32 = jnp.float32
BF16 = jnp.bfloat16


def sin_pi(fraction):
    square = fraction * fraction
    total = jnp.full_like(square, SIN_PI[4])
    for coefficient in SIN_PI[3::-1]:
        total = total * square + coefficient
    return total * fraction


def dot_nn(left, right):
    return lax.dot_general(left, right, (((1,), (0,)), ((), ())), preferred_element_type=F32)


def dot_nt(left, right):
    return lax.dot_general(left, right, (((1,), (1,)), ((), ())), preferred_element_type=F32)


def rank_tables(me, dev, slot, cuts, tables):
    slices = dev.shape[1]
    per_block = slices // cuts
    source = lax.broadcasted_iota(jnp.int32, (cuts, slices), 0)
    low = lax.broadcasted_iota(jnp.int32, (slices, slices), 0)
    high = lax.broadcasted_iota(jnp.int32, (slices, slices), 1)
    same = low // per_block == high // per_block
    block = jnp.where(same, 1.0, 0.0).astype(BF16)
    before = jnp.where(same & (low < high), 1.0, 0.0).astype(BF16)
    hit0 = jnp.where(dev[0:1] == source, 1.0, 0.0)
    hit1 = jnp.where(dev[1:2] == source, 1.0, 0.0)
    rank0 = dot_nn(hit0.astype(BF16), before)
    rank1 = dot_nn(hit1.astype(BF16), before) + dot_nn(hit0.astype(BF16), block)
    rank0 = jnp.sum(hit0 * rank0, axis=0, keepdims=True)
    rank1 = jnp.sum(hit1 * rank1, axis=0, keepdims=True)
    arrival0 = dev[0:1] * CAP + rank0.astype(jnp.int32)
    arrival1 = dev[1:2] * CAP + rank1.astype(jnp.int32)
    tables[0:1, :] = arrival0
    tables[1:2, :] = arrival1
    wanted = lax.broadcasted_iota(jnp.int32, (8, slices), 0).astype(F32)
    mine0 = (dev[0:1] == me) & (rank0 == wanted)
    mine1 = (dev[1:2] == me) & (rank1 == wanted)
    slots = jnp.where(mine0, slot[0:1].astype(F32), 0.0) + jnp.where(mine1, slot[1:2].astype(F32), 0.0)
    place = lax.broadcasted_iota(jnp.int32, (slices, LANES), 0) // per_block
    column = lax.broadcasted_iota(jnp.int32, (slices, LANES), 1)
    chosen = dot_nn(slots.astype(BF16), jnp.where(place == column, 1.0, 0.0).astype(BF16))
    tables[8:16, 0:LANES] = chosen.astype(jnp.int32)


def section_kernel(
    cuts,
    tiles,
    theta_hbm,
    dev_hbm,
    slot_hbm,
    weight_hbm,
    coupling_hbm,
    field_hbm,
    prop_hbm,
    cellx_hbm,
    celly_hbm,
    out_hbm,
    theta_ref,
    dev_ref,
    slot_ref,
    weight_ref,
    coupling_ref,
    field_v,
    prop_v,
    cellx_v,
    celly_v,
    tables_v,
    tables_s,
    phase_v,
    outgoing,
    arrived,
    row_code,
    col_code,
    full,
    field_send,
    source_send,
    field_hop,
    source_hop,
    field_recv,
    near_recv,
    far_recv,
    tall,
    diff,
    back_send,
    back_recv,
    local_sem,
    theta_ss,
    theta_rs,
    field_ss,
    field_rs,
    near_ss,
    near_rs,
    far_ss,
    far_rs,
    twin_ss,
    hop_ss,
    hop_rs,
    back_ss,
    back_rs,
):
    c = lax.axis_index("cuts")
    t = lax.axis_index("tile")
    slots = theta_ref.shape[0]
    share = theta_ref.shape[1]
    pieces = share // LANES
    grid = prop_v.shape[1]
    rows = grid // tiles
    parts = 2 * rows
    columns = grid // LANES
    groups = tiles // 4
    field_rows = 2 * slots * rows

    first = [
        pltpu.make_async_copy(dev_hbm, dev_ref, local_sem.at[0]),
        pltpu.make_async_copy(slot_hbm, slot_ref, local_sem.at[1]),
        pltpu.make_async_copy(theta_hbm, theta_ref, local_sem.at[2]),
        pltpu.make_async_copy(weight_hbm, weight_ref, local_sem.at[3]),
        pltpu.make_async_copy(coupling_hbm, coupling_ref, local_sem.at[4]),
        pltpu.make_async_copy(cellx_hbm, cellx_v, local_sem.at[5]),
        pltpu.make_async_copy(celly_hbm, celly_v, local_sem.at[6]),
        pltpu.make_async_copy(prop_hbm, prop_v, local_sem.at[7]),
    ]
    field_loads = [
        pltpu.make_async_copy(
            field_hbm.at[:, pl.ds(q * LANES, LANES)], field_v.at[q, pl.ds(0, field_rows)], local_sem.at[8 + q]
        )
        for q in range(columns)
    ]
    for load in first + field_loads:
        load.start()
    barrier = pltpu.get_barrier_semaphore()

    def greet_cut(step, carry):
        pl.semaphore_signal(barrier, inc=1, device_id=(lax.rem(c + step, cuts), t), device_id_type=MESH)
        return carry

    def greet_tile(step, carry):
        pl.semaphore_signal(barrier, inc=1, device_id=(c, lax.rem(t + step, tiles)), device_id_type=MESH)
        return carry

    lax.fori_loop(1, cuts, greet_cut, 0)
    lax.fori_loop(1, tiles, greet_tile, 0)

    first[0].wait()
    first[1].wait()
    rank_tables(c, dev_ref[...], slot_ref[...], cuts, tables_v)
    to_scalar = pltpu.make_async_copy(tables_v, tables_s, local_sem.at[11])
    to_scalar.start()

    first[2].wait()
    turns = theta_ref[...] * (HARM / (2.0 * math.pi))
    turns = turns - jnp.floor(turns + 0.5)
    turns = jnp.minimum(jnp.floor(turns * 65536.0 + 0.5), 32767.0)
    for piece in range(pieces):
        phase_v[:, piece, :] = turns[:, piece * LANES : (piece + 1) * LANES]
    def hop_copy(which, src, dst):
        return pltpu.make_async_remote_copy(
            src_ref=src,
            dst_ref=dst,
            send_sem=hop_ss.at[which],
            recv_sem=hop_rs.at[which],
            device_id=(lax.rem(c + 1, cuts), t),
            device_id_type=MESH,
        )

    def block_copy(src, dst, to, send, recv):
        return pltpu.make_async_remote_copy(
            src_ref=src, dst_ref=dst, send_sem=send, recv_sem=recv, device_id=(c, to), device_id_type=MESH
        )

    def deliver(src, dst, to, send, recv):
        @pl.when(to == t)
        def _():
            pltpu.make_async_copy(src, dst.at[t], recv.at[t]).start()

        @pl.when(to != t)
        def _():
            block_copy(src, dst.at[t], to, send.at[to], recv.at[t]).start()

    def arrive(dst, other, recv):
        block_copy(back_send.at[0], dst.at[other], other, back_ss.at[0], recv.at[other]).wait_recv()

    def stage_field(slot):
        pieces_re = [field_v[q, pl.ds(slot, rows, stride=2 * slots), :] for q in range(columns)]
        pieces_im = [field_v[q, pl.ds(slot + slots, rows, stride=2 * slots), :] for q in range(columns)]
        field_send[slot] = jnp.concatenate(
            [jnp.concatenate(pieces_re, 1), jnp.concatenate(pieces_im, 1)], 0
        ).astype(BF16)

    for load in field_loads:
        load.wait()
    stage_field(slots - 2)
    stage_field(slots - 1)
    pl.semaphore_wait(barrier, cuts + tiles - 2)
    for which in range(2):
        hop_copy(which, field_send.at[slots - 2 + which], field_hop.at[which]).start()
    to_scalar.wait()

    def pick(block, carry):
        for rank in range(CAP):
            chosen = jnp.clip(tables_s[8 + rank, block], 0, slots - 1)
            outgoing[block * CAP + rank] = phase_v[chosen].astype(jnp.int32).astype(jnp.int16)
        return carry

    lax.fori_loop(0, cuts, pick, 0)

    def theta_copy(to, slot_of, sem_of):
        return pltpu.make_async_remote_copy(
            src_ref=outgoing.at[pl.ds(to * CAP, CAP)],
            dst_ref=arrived.at[pl.ds(slot_of * CAP, CAP)],
            send_sem=theta_ss.at[to],
            recv_sem=theta_rs.at[sem_of],
            device_id=(to, t),
            device_id_type=MESH,
        )

    def theta_start(step, carry):
        theta_copy(lax.rem(c + step, cuts), c, c).start()
        return carry

    lax.fori_loop(1, cuts, theta_start, 0)
    own_theta = pltpu.make_async_copy(
        outgoing.at[pl.ds(c * CAP, CAP)], arrived.at[pl.ds(c * CAP, CAP)], theta_rs.at[c]
    )
    own_theta.start()

    def one_field(step, carry):
        slot = lax.rem(t + step, slots - 2)
        stage_field(slot)
        deliver(field_send.at[slot], field_recv, slot + 2, field_ss, field_rs)
        return carry

    lax.fori_loop(0, slots - 2, one_field, 0)
    for which in range(2):
        hop_copy(which, field_send.at[0], field_hop.at[which]).wait_recv()
        deliver(field_hop.at[which], field_recv, which, field_ss, field_rs)

    for load in first[3:]:
        load.wait()

    def codes(index, carry):
        cell_x = cellx_v[index]
        cell_y = celly_v[index]
        code = (cell_y // LANES) * rows + cell_x
        column = cell_y % LANES
        for k in range(2):
            row_code[2 * index + k] = jnp.broadcast_to(code[k : k + 1].astype(F32), (16, share)).astype(BF16)
            col_code[2 * index + k] = jnp.broadcast_to(column[k : k + 1].astype(F32), (16, share)).astype(BF16)
        return carry

    lax.fori_loop(0, slots, codes, 0)
    full[0:grid, 0:grid] = prop_v[0]
    full[0:grid, grid:] = -prop_v[1]
    full[grid:, 0:grid] = prop_v[1]
    full[grid:, grid:] = prop_v[0]

    own_theta.wait()

    def theta_end(step, carry):
        other = lax.rem(c + step, cuts)
        theta_copy(other, other, other).wait_recv()
        return carry

    lax.fori_loop(1, cuts, theta_end, 0)

    width = 4 * LANES
    subs = lax.broadcasted_iota(jnp.int32, (16, width), 0)
    levels = [(subs + 16 * level).astype(F32).astype(BF16) for level in range(8)]
    one = jnp.ones((16, width), BF16)
    zero = jnp.zeros((16, width), BF16)
    c0r, c0i = coupling_ref[0, 0], coupling_ref[0, 1]
    c1r, c1i = coupling_ref[1, 0], coupling_ref[1, 1]

    def deposit(slot):
        total = None
        for k in range(2):
            entry = c * slots + slot
            row = jnp.clip(tables_s[k, entry], 0, cuts * CAP - 1)
            weight = weight_ref[k, entry]
            phase = arrived[row].astype(jnp.int32).astype(F32) * (1.0 / 32768.0)
            cosine = sin_pi(0.5 - jnp.abs(phase))
            sine = sin_pi(jnp.maximum(jnp.minimum(phase, 1.0 - phase), -1.0 - phase))
            value_re = weight * cosine
            value_im = weight * sine
            index = 2 * slot + k
            for group in range(pieces // 4):
                lanes = slice(group * width, (group + 1) * width)
                column = col_code[index, :, lanes]
                code = row_code[index, :, lanes]
                spread_re = jnp.concatenate(
                    [jnp.broadcast_to(value_re[4 * group + i : 4 * group + i + 1], (16, LANES)) for i in range(4)], 1
                ).astype(BF16)
                spread_im = jnp.concatenate(
                    [jnp.broadcast_to(value_im[4 * group + i : 4 * group + i + 1], (16, LANES)) for i in range(4)], 1
                ).astype(BF16)
                hits = [code == level for level in levels[:5]]
                left = jnp.concatenate(
                    [jnp.where(hit, spread_re, zero) for hit in hits]
                    + [jnp.where(hit, spread_im, zero) for hit in hits],
                    0,
                )
                right = jnp.concatenate([jnp.where(column == level, one, zero) for level in levels], 0)
                product = dot_nt(left, right)
                total = product if total is None else total + product
        real_part = jnp.concatenate([total[i * rows : (i + 1) * rows] for i in range(3)], 1)
        imag_part = jnp.concatenate([total[80 + i * rows : 80 + (i + 1) * rows] for i in range(3)], 1)
        source_send[slot] = jnp.concatenate([real_part, imag_part], 0).astype(BF16)

    deposit(slots - 1)
    hop_copy(3, source_send.at[slots - 1], source_hop.at[1]).start()
    deposit(slots - 2)
    hop_copy(2, source_send.at[slots - 2], source_hop.at[0]).start()
    deliver(source_send.at[slots - 2], near_recv, slots - 1, near_ss, near_rs)

    def one_slot(step, carry):
        slot = lax.rem(t + step, slots - 2)
        deposit(slot)
        deliver(source_send.at[slot], near_recv, slot + 1, near_ss, near_rs)

        @pl.when(lax.rem(slot, 2) == 0)
        def _():
            deliver(source_send.at[slot], far_recv, slot + 2, far_ss, far_rs)

        @pl.when(step == 4)
        def _():
            hop_copy(3, source_send.at[0], source_hop.at[1]).wait_recv()
            deliver(source_hop.at[1], near_recv, 0, near_ss, near_rs)
            hop_copy(2, source_send.at[0], source_hop.at[0]).wait_recv()
            deliver(source_hop.at[0], far_recv, 0, far_ss, far_rs)

        return carry

    lax.fori_loop(0, slots - 2, one_slot, 0)

    def field_in(other, carry):
        arrive(field_recv, other, field_rs)
        return carry

    lax.fori_loop(0, tiles, field_in, 0)
    even = lax.rem(t, 2) == 0
    twin = t + 1 - 2 * lax.rem(t, 2)

    def pair_of(ref, pair):
        first = ref[2 * pair].astype(F32)
        second = ref[2 * pair + 1].astype(F32)
        real_part = jnp.concatenate([first[:rows], second[:rows]], 0)
        imag_part = jnp.concatenate([first[rows:], second[rows:]], 0)
        return real_part, imag_part

    def first_period(step, carry):
        group = lax.rem((t + tiles - 1) // 4 + groups - step, groups)
        for i in range(3, -1, -1):
            other = 4 * group + i
            arrive(near_recv, other, near_rs)

            @pl.when(even)
            def _():
                block_copy(
                    near_recv.at[other], far_recv.at[other], twin, twin_ss.at[other], far_rs.at[other]
                ).start()

        for i in range(3, -1, -1):
            arrive(far_recv, 4 * group + i, far_rs)
        blocks = []
        for i in range(2):
            field_re, field_im = pair_of(field_recv, 2 * group + i)
            source_re, source_im = pair_of(far_recv, 2 * group + i)
            sum_re = field_re + c0r * source_re - c0i * source_im
            sum_im = field_im + c0r * source_im + c0i * source_re
            blocks.append(jnp.concatenate([sum_re.astype(BF16), sum_im.astype(BF16)], 1))
        inter = dot_nt(jnp.concatenate(blocks, 0), full[...])
        start = pl.multiple_of(group * 4 * rows, 4 * rows)
        tall[pl.ds(start, 4 * rows), :] = inter[:, 0:grid].astype(BF16)
        tall[pl.ds(grid + start, 4 * rows), :] = inter[:, grid:].astype(BF16)
        return carry

    lax.fori_loop(0, groups, first_period, 0)
    diff[...] = dot_nn(full[...], tall[...])
    for pair in range(tiles // 2):
        real_part, imag_part = pair_of(near_recv, pair)
        top = slice(pair * parts, (pair + 1) * parts)
        low = slice(grid + pair * parts, grid + (pair + 1) * parts)
        tall[top, :] = (diff[top, :] + c1r * real_part - c1i * imag_part).astype(BF16)
        tall[low, :] = (diff[low, :] + c1r * imag_part + c1i * real_part).astype(BF16)

    def chunk_out(step, carry):
        chunk = lax.rem(t // 4 + step, groups)
        start = pl.multiple_of(chunk * 4 * rows, 4 * rows)
        inter_re = dot_nn(full[pl.ds(start, 4 * rows), :], tall[...])
        inter_im = dot_nn(full[pl.ds(start + grid, 4 * rows), :], tall[...])
        for i in range(4):
            to = 4 * chunk + i
            back_send[to] = jnp.concatenate(
                [inter_re[i * rows : (i + 1) * rows], inter_im[i * rows : (i + 1) * rows]], 0
            ).astype(BF16)
            deliver(back_send.at[to], back_recv, to, back_ss, back_rs)
        return carry

    lax.fori_loop(0, groups, chunk_out, 0)

    def last_period(step, carry):
        group = lax.rem(t // 4 + groups - step, groups)
        blocks = []
        for i in range(4):
            arrive(back_recv, 4 * group + i, back_rs)
        for i in range(2):
            real_part, imag_part = pair_of(back_recv, 2 * group + i)
            blocks.append(jnp.concatenate([real_part.astype(BF16), imag_part.astype(BF16)], 1))
        result = dot_nt(jnp.concatenate(blocks, 0), full[...])
        for i in range(4):
            slot = 4 * group + i
            for q in range(columns):
                for part in range(2):
                    at = part * grid + q * LANES
                    field_v[q, pl.ds(part * slots + slot, rows, stride=2 * slots), :] = result[
                        i * rows : (i + 1) * rows, at : at + LANES
                    ]
        return carry

    lax.fori_loop(0, groups, last_period, 0)
    stores = [
        pltpu.make_async_copy(
            field_v.at[q, pl.ds(0, field_rows)], out_hbm.at[:, pl.ds(q * LANES, LANES)], local_sem.at[8 + q]
        )
        for q in range(columns)
    ]
    for store in stores:
        store.start()

    def sent_theta(step, carry):
        other = lax.rem(c + step, cuts)
        theta_copy(other, other, other).wait_send()
        return carry

    lax.fori_loop(1, cuts, sent_theta, 0)

    def leave(to, send):
        block_copy(back_send.at[0], back_recv.at[0], to, send.at[to], back_rs.at[0]).wait_send()

    def sent(step, carry):
        other = lax.rem(t + step, tiles)
        leave(other, field_ss)
        leave(other, near_ss)
        leave(other, back_ss)

        @pl.when(lax.rem(other, 2) == 0)
        def _():
            leave(other, far_ss)

        return carry

    lax.fori_loop(1, tiles, sent, 0)

    @pl.when(even)
    def _():
        def sent_twin(other, carry):
            leave(other, twin_ss)
            return carry

        lax.fori_loop(0, tiles, sent_twin, 0)

    for which in range(2):
        hop_copy(which, field_send.at[0], field_hop.at[which]).wait_send()
        hop_copy(2 + which, source_send.at[0], source_hop.at[which]).wait_send()
    for store in stores:
        store.wait()


def on_device(cuts, tiles, field_in, propagator, theta, cell_x, cell_y, src_dev, src_slot, weights, coupling):
    grid = propagator.shape[1]
    rows = grid // tiles
    slots, share = theta.shape
    slices = src_dev.shape[0]
    hbm = pl.BlockSpec(memory_space=pltpu.HBM)
    block = (2 * rows, grid)
    blocks = pltpu.VMEM((tiles,) + block, BF16)
    dma = pltpu.SemaphoreType.DMA
    result = pl.pallas_call(
        functools.partial(section_kernel, cuts, tiles),
        out_shape=jax.ShapeDtypeStruct((rows * 2 * slots, grid), F32),
        in_specs=[hbm] * 9,
        out_specs=hbm,
        scratch_shapes=[
            pltpu.VMEM((slots, share), F32),
            pltpu.VMEM((2, slices), jnp.int32),
            pltpu.VMEM((2, slices), jnp.int32),
            pltpu.SMEM((2, slices), F32),
            pltpu.SMEM((2, 2), F32),
            pltpu.VMEM((grid // LANES, (rows + 1) * 2 * slots, LANES), F32),
            pltpu.VMEM((2, grid, grid), BF16),
            pltpu.VMEM((slots, 2, share), jnp.int32),
            pltpu.VMEM((slots, 2, share), jnp.int32),
            pltpu.VMEM((16, slices), jnp.int32),
            pltpu.SMEM((16, slices), jnp.int32),
            pltpu.VMEM((slots, share // LANES, LANES), F32),
            pltpu.VMEM((cuts * CAP, share // LANES, LANES), jnp.int16),
            pltpu.VMEM((cuts * CAP, share // LANES, LANES), jnp.int16),
            pltpu.VMEM((2 * slots, 16, share), BF16),
            pltpu.VMEM((2 * slots, 16, share), BF16),
            pltpu.VMEM((2 * grid, 2 * grid), BF16),
            blocks,
            blocks,
            pltpu.VMEM((2,) + block, BF16),
            pltpu.VMEM((2,) + block, BF16),
            blocks,
            blocks,
            blocks,
            pltpu.VMEM((2 * grid, grid), BF16),
            pltpu.VMEM((2 * grid, grid), F32),
            blocks,
            blocks,
            dma((12,)),
            dma((cuts,)),
            dma((cuts,)),
            dma((tiles,)),
            dma((tiles,)),
            dma((tiles,)),
            dma((tiles,)),
            dma((tiles,)),
            dma((tiles,)),
            dma((tiles,)),
            dma((4,)),
            dma((4,)),
            dma((tiles,)),
            dma((tiles,)),
        ],
        compiler_params=pltpu.CompilerParams(
            collective_id=0, has_side_effects=True, vmem_limit_bytes=64 * 1024 * 1024
        ),
    )(
        theta,
        src_dev.T,
        src_slot.T,
        weights.T,
        coupling,
        field_in.reshape(rows * 2 * slots, grid),
        propagator,
        cell_x,
        cell_y,
    )
    return result.reshape(rows, 2, slots, grid)


def solution(mesh):
    in_specs = (
        P("tile", None, "cuts", None),
        P(),
        P("cuts", "tile"),
        P("cuts", None, "tile"),
        P("cuts", None, "tile"),
        P(),
        P(),
        P(),
        P(),
    )
    out_specs = P("tile", None, "cuts", None)
    run = functools.partial(on_device, mesh.shape["cuts"], mesh.shape["tile"])
    return jax.shard_map(run, mesh=mesh, in_specs=in_specs, out_specs=out_specs, check_vma=False)
```

time: 62.1 us -> 55.8 us (0.90)
  local copies, waits for them, and re-layouts: 7.86 us -> 2.36 us
    unnamed x18 -> x1, local copies, waits for them, and re-layouts: 7.86 us -> 2.36 us
    pallas_call x1 -> x0, Pallas kernels: 1.91 us -> none  [on_device(): pl.pallas_call(final_kernel, out_shape=jax.ShapeDtypeStruct((rows, 2, slo...]
    pallas_call x1, Pallas kernels: 52 us -> 53.3 us  [on_device(): pl.pallas_call(functools.partial(section_kernel, cuts, tiles), out_shape=...]
where the time goes in v1:
time: 55.8 us; the launch traced here: 55.7 us
  Pallas kernels  53.3 us (96%)
  local copies, waits for them, and re-layouts  2.36 us (4%)
    pallas_call x1, Pallas kernels, on_device(): pl.pallas_call(functools.partial(section_kernel, cuts, tiles), out_shape=...  53.3 us
    unnamed x1, local copies, waits for them, and re-layouts  2.36 us

profile of v1, /device:TPU:1, one launch (start us, length us, event | category | flops | bytes accessed | tf_op | source)
XLA Modules:
  0.0 55.7 jit_solution(4790678180460469240)
XLA Ops:
  0.0 53.3 %shard_map.91 = f32[768,384]{1,0:T(8,128)} custom-call(f32[16,2048]{1,0:T(8,128)} %theta_hbm.1, s32[2,256]{1,0:T(2,128)} %bitcast.7, s32[2,256]{1,0:T(2,128)} %bitcast.8, f32[2,256]{1,0:T(2,128)} %bitcast.9, f32[2,2]{1,0:T(2,128)} %coupling_hbm.1, f32[768,384]{1,0:T(8,128)} %bitcast.6, bf16[2,384,384]{2,1,0:T(8,128)(2,1)} %prop_hbm.1, ...), custom_call_target="tpu_custom_call" | custom-call | tf_op jit(solution)/shard_map/pallas_call | solution.py:504
  53.3 2.4 %copy.11 = f32[24,2,16,384]{3,2,1,0:T(8,128)} copy(f32[24,2,16,384]{3,2,1,0:T(8,128)} %bitcast.5) | data formatting | bytes 2359296

commit v2 on v1

--- a/solution.py
+++ b/solution.py
@@ -29,6 +29,10 @@
     for coefficient in SIN_PI[3::-1]:
         total = total * square + coefficient
     return total * fraction
+
+
+def turn(step, count):
+    return count // 2 + (1 - 2 * lax.rem(step, 2)) * ((step + 1) // 2)
 
 
 def dot_nn(left, right):
@@ -166,6 +170,9 @@
 
     lax.fori_loop(1, cuts, greet_cut, 0)
     lax.fori_loop(1, tiles, greet_tile, 0)
+    pl.semaphore_signal(
+        barrier, inc=1, device_id=(lax.rem(c + cuts - 1, cuts), tiles - 1), device_id_type=MESH
+    )
 
     first[0].wait()
     first[1].wait()
@@ -194,14 +201,14 @@
             src_ref=src, dst_ref=dst, send_sem=send, recv_sem=recv, device_id=(c, to), device_id_type=MESH
         )
 
-    def deliver(src, dst, to, send, recv):
+    def deliver(src, dst, to, send, recv, place=t):
         @pl.when(to == t)
         def _():
-            pltpu.make_async_copy(src, dst.at[t], recv.at[t]).start()
+            pltpu.make_async_copy(src, dst.at[place], recv.at[place]).start()
 
         @pl.when(to != t)
         def _():
-            block_copy(src, dst.at[t], to, send.at[to], recv.at[t]).start()
+            block_copy(src, dst.at[place], to, send.at[to], recv.at[place]).start()
 
     def arrive(dst, other, recv):
         block_copy(back_send.at[0], dst.at[other], other, back_ss.at[0], recv.at[other]).wait_recv()
@@ -215,11 +222,9 @@
 
     for load in field_loads:
         load.wait()
-    stage_field(slots - 2)
     stage_field(slots - 1)
-    pl.semaphore_wait(barrier, cuts + tiles - 2)
-    for which in range(2):
-        hop_copy(which, field_send.at[slots - 2 + which], field_hop.at[which]).start()
+    pl.semaphore_wait(barrier, cuts + tiles - 2 + tiles * (t // (tiles - 1)))
+    hop_copy(0, field_send.at[slots - 1], field_hop.at[0]).start()
     to_scalar.wait()
 
     def pick(block, carry):
@@ -251,15 +256,18 @@
     own_theta.start()
 
     def one_field(step, carry):
-        slot = lax.rem(t + step, slots - 2)
-        stage_field(slot)
-        deliver(field_send.at[slot], field_recv, slot + 2, field_ss, field_rs)
-        return carry
-
-    lax.fori_loop(0, slots - 2, one_field, 0)
-    for which in range(2):
-        hop_copy(which, field_send.at[0], field_hop.at[which]).wait_recv()
-        deliver(field_hop.at[which], field_recv, which, field_ss, field_rs)
+        slot = lax.rem(t + turn(step, slots), slots)
+
+        @pl.when(slot < slots - 1)
+        def _():
+            stage_field(slot)
+            deliver(field_send.at[slot], field_recv, slot + 1, field_ss, field_rs)
+
+        return carry
+
+    lax.fori_loop(0, slots, one_field, 0)
+    hop_copy(0, field_send.at[0], field_hop.at[0]).wait_recv()
+    deliver(field_hop.at[0], field_recv, 0, field_ss, field_rs)
 
     for load in first[3:]:
         load.wait()
@@ -333,38 +341,36 @@
         source_send[slot] = jnp.concatenate([real_part, imag_part], 0).astype(BF16)
 
     deposit(slots - 1)
-    hop_copy(3, source_send.at[slots - 1], source_hop.at[1]).start()
-    deposit(slots - 2)
-    hop_copy(2, source_send.at[slots - 2], source_hop.at[0]).start()
-    deliver(source_send.at[slots - 2], near_recv, slots - 1, near_ss, near_rs)
+    hop_copy(1, source_send.at[slots - 1], source_hop.at[0]).start()
+    deliver(source_send.at[slots - 1], near_recv, slots - 1, near_ss, near_rs)
 
     def one_slot(step, carry):
-        slot = lax.rem(t + step, slots - 2)
-        deposit(slot)
-        deliver(source_send.at[slot], near_recv, slot + 1, near_ss, near_rs)
-
-        @pl.when(lax.rem(slot, 2) == 0)
+        slot = lax.rem(t + turn(step, slots), slots)
+
+        @pl.when(slot < slots - 1)
         def _():
-            deliver(source_send.at[slot], far_recv, slot + 2, far_ss, far_rs)
+            deposit(slot)
+            deliver(source_send.at[slot], far_recv, slot + 1, far_ss, far_rs)
+
+        @pl.when((lax.rem(slot, 2) == 1) & (slot < slots - 1))
+        def _():
+            deliver(source_send.at[slot], near_recv, slot, near_ss, near_rs)
 
         @pl.when(step == 4)
         def _():
-            hop_copy(3, source_send.at[0], source_hop.at[1]).wait_recv()
-            deliver(source_hop.at[1], near_recv, 0, near_ss, near_rs)
-            hop_copy(2, source_send.at[0], source_hop.at[0]).wait_recv()
+            hop_copy(1, source_send.at[0], source_hop.at[0]).wait_recv()
             deliver(source_hop.at[0], far_recv, 0, far_ss, far_rs)
 
         return carry
 
-    lax.fori_loop(0, slots - 2, one_slot, 0)
+    lax.fori_loop(0, slots, one_slot, 0)
 
     def field_in(other, carry):
         arrive(field_recv, other, field_rs)
         return carry
 
     lax.fori_loop(0, tiles, field_in, 0)
-    even = lax.rem(t, 2) == 0
-    twin = t + 1 - 2 * lax.rem(t, 2)
+    odd = lax.rem(t, 2) == 1
 
     def pair_of(ref, pair):
         first = ref[2 * pair].astype(F32)
@@ -374,19 +380,17 @@
         return real_part, imag_part
 
     def first_period(step, carry):
-        group = lax.rem((t + tiles - 1) // 4 + groups - step, groups)
-        for i in range(3, -1, -1):
+        group = lax.rem(t // 4 + turn(step, groups), groups)
+        for i in range(4):
             other = 4 * group + i
-            arrive(near_recv, other, near_rs)
-
-            @pl.when(even)
+            arrive(far_recv, other, far_rs)
+
+            @pl.when(odd)
             def _():
                 block_copy(
-                    near_recv.at[other], far_recv.at[other], twin, twin_ss.at[other], far_rs.at[other]
+                    far_recv.at[other], near_recv.at[other], t - 1, twin_ss.at[other], near_rs.at[other]
                 ).start()
 
-        for i in range(3, -1, -1):
-            arrive(far_recv, 4 * group + i, far_rs)
         blocks = []
         for i in range(2):
             field_re, field_im = pair_of(field_recv, 2 * group + i)
@@ -402,6 +406,12 @@
 
     lax.fori_loop(0, groups, first_period, 0)
     diff[...] = dot_nn(full[...], tall[...])
+
+    def near_in(other, carry):
+        arrive(near_recv, other, near_rs)
+        return carry
+
+    lax.fori_loop(0, tiles, near_in, 0)
     for pair in range(tiles // 2):
         real_part, imag_part = pair_of(near_recv, pair)
         top = slice(pair * parts, (pair + 1) * parts)
@@ -410,7 +420,7 @@
         tall[low, :] = (diff[low, :] + c1r * imag_part + c1i * real_part).astype(BF16)
 
     def chunk_out(step, carry):
-        chunk = lax.rem(t // 4 + step, groups)
+        chunk = lax.rem(t // 4 + turn(step, groups), groups)
         start = pl.multiple_of(chunk * 4 * rows, 4 * rows)
         inter_re = dot_nn(full[pl.ds(start, 4 * rows), :], tall[...])
         inter_im = dot_nn(full[pl.ds(start + grid, 4 * rows), :], tall[...])
@@ -419,13 +429,28 @@
             back_send[to] = jnp.concatenate(
                 [inter_re[i * rows : (i + 1) * rows], inter_im[i * rows : (i + 1) * rows]], 0
             ).astype(BF16)
-            deliver(back_send.at[to], back_recv, to, back_ss, back_rs)
+
+            @pl.when(t < tiles - 1)
+            def _():
+                deliver(back_send.at[to], back_recv, to, back_ss, back_rs, t + 1)
+
+            @pl.when(t == tiles - 1)
+            def _():
+                pltpu.make_async_remote_copy(
+                    src_ref=back_send.at[to],
+                    dst_ref=back_recv.at[0],
+                    send_sem=back_ss.at[to],
+                    recv_sem=back_rs.at[0],
+                    device_id=(lax.rem(c + 1, cuts), to),
+                    device_id_type=MESH,
+                ).start()
+
         return carry
 
     lax.fori_loop(0, groups, chunk_out, 0)
 
     def last_period(step, carry):
-        group = lax.rem(t // 4 + groups - step, groups)
+        group = lax.rem(t // 4 + turn(step, groups), groups)
         blocks = []
         for i in range(4):
             arrive(back_recv, 4 * group + i, back_rs)
@@ -466,18 +491,18 @@
     def sent(step, carry):
         other = lax.rem(t + step, tiles)
         leave(other, field_ss)
-        leave(other, near_ss)
+        leave(other, far_ss)
         leave(other, back_ss)
 
-        @pl.when(lax.rem(other, 2) == 0)
+        @pl.when(lax.rem(other, 2) == 1)
         def _():
-            leave(other, far_ss)
+            leave(other, near_ss)
 
         return carry
 
     lax.fori_loop(1, tiles, sent, 0)
 
-    @pl.when(even)
+    @pl.when(odd)
     def _():
         def sent_twin(other, carry):
             leave(other, twin_ss)
@@ -485,9 +510,13 @@
 
         lax.fori_loop(0, tiles, sent_twin, 0)
 
-    for which in range(2):
-        hop_copy(which, field_send.at[0], field_hop.at[which]).wait_send()
-        hop_copy(2 + which, source_send.at[0], source_hop.at[which]).wait_send()
+    hop_copy(0, field_send.at[0], field_hop.at[0]).wait_send()
+    hop_copy(1, source_send.at[0], source_hop.at[0]).wait_send()
+
+    @pl.when(t == tiles - 1)
+    def _():
+        leave(t, back_ss)
+
     for store in stores:
         store.wait()
 
@@ -526,8 +555,8 @@
             pltpu.VMEM((2 * grid, 2 * grid), BF16),
             blocks,
             blocks,
-            pltpu.VMEM((2,) + block, BF16),
-            pltpu.VMEM((2,) + block, BF16),
+            pltpu.VMEM((1,) + block, BF16),
+            pltpu.VMEM((1,) + block, BF16),
             blocks,
             blocks,
             blocks,
@@ -545,8 +574,8 @@
             dma((tiles,)),
             dma((tiles,)),
             dma((tiles,)),
-            dma((4,)),
-            dma((4,)),
+            dma((2,)),
+            dma((2,)),
             dma((tiles,)),
             dma((tiles,)),
         ],

time: 55.8 us -> 54 us (0.968)
  Pallas kernels: 53.3 us -> 51.5 us
    pallas_call x1, Pallas kernels: 53.3 us -> 51.5 us  [on_device(): pl.pallas_call(functools.partial(section_kernel, cuts, tiles), out_shape=...]
where the time goes in v2:
time: 54 us; the launch traced here: 53.9 us
  Pallas kernels  51.5 us (95%)
  local copies, waits for them, and re-layouts  2.36 us (4%)
    pallas_call x1, Pallas kernels, on_device(): pl.pallas_call(functools.partial(section_kernel, cuts, tiles), out_shape=...  51.5 us
    unnamed x1, local copies, waits for them, and re-layouts  2.36 us

profile of v2, /device:TPU:1, one launch (start us, length us, event | category | flops | bytes accessed | tf_op | source)
XLA Modules:
  0.0 53.9 jit_solution(18037810671380896081)
XLA Ops:
  0.0 51.5 %shard_map.91 = f32[768,384]{1,0:T(8,128)} custom-call(f32[16,2048]{1,0:T(8,128)} %theta_hbm.1, s32[2,256]{1,0:T(2,128)} %bitcast.7, s32[2,256]{1,0:T(2,128)} %bitcast.8, f32[2,256]{1,0:T(2,128)} %bitcast.9, f32[2,2]{1,0:T(2,128)} %coupling_hbm.1, f32[768,384]{1,0:T(8,128)} %bitcast.6, bf16[2,384,384]{2,1,0:T(8,128)(2,1)} %prop_hbm.1, ...), custom_call_target="tpu_custom_call" | custom-call | tf_op jit(solution)/shard_map/pallas_call | solution.py:533
  51.5 2.4 %copy.11 = f32[24,2,16,384]{3,2,1,0:T(8,128)} copy(f32[24,2,16,384]{3,2,1,0:T(8,128)} %bitcast.5) | data formatting | bytes 2359296

commit v3 on v2

--- a/solution.py
+++ b/solution.py
@@ -84,14 +84,14 @@
     prop_hbm,
     cellx_hbm,
     celly_hbm,
-    out_hbm,
+    wide_ref,
+    prop_v,
     theta_ref,
     dev_ref,
     slot_ref,
     weight_ref,
     coupling_ref,
     field_v,
-    prop_v,
     cellx_v,
     celly_v,
     tables_v,
@@ -449,34 +449,24 @@
 
     lax.fori_loop(0, groups, chunk_out, 0)
 
-    def last_period(step, carry):
+    def gather(step, carry):
         group = lax.rem(t // 4 + turn(step, groups), groups)
-        blocks = []
-        for i in range(4):
-            arrive(back_recv, 4 * group + i, back_rs)
-        for i in range(2):
-            real_part, imag_part = pair_of(back_recv, 2 * group + i)
-            blocks.append(jnp.concatenate([real_part.astype(BF16), imag_part.astype(BF16)], 1))
-        result = dot_nt(jnp.concatenate(blocks, 0), full[...])
         for i in range(4):
             slot = 4 * group + i
+            arrive(back_recv, slot, back_rs)
+            block = back_recv[slot].astype(F32)
             for q in range(columns):
                 for part in range(2):
-                    at = part * grid + q * LANES
-                    field_v[q, pl.ds(part * slots + slot, rows, stride=2 * slots), :] = result[
-                        i * rows : (i + 1) * rows, at : at + LANES
+                    field_v[q, pl.ds(part * grid + slot, rows, stride=slots), :] = block[
+                        part * rows : (part + 1) * rows, q * LANES : (q + 1) * LANES
                     ]
         return carry
 
-    lax.fori_loop(0, groups, last_period, 0)
-    stores = [
-        pltpu.make_async_copy(
-            field_v.at[q, pl.ds(0, field_rows)], out_hbm.at[:, pl.ds(q * LANES, LANES)], local_sem.at[8 + q]
-        )
-        for q in range(columns)
-    ]
-    for store in stores:
-        store.start()
+    lax.fori_loop(0, groups, gather, 0)
+    for q in range(columns):
+        for part in range(2):
+            at = part * grid + q * LANES
+            wide_ref[:, at : at + LANES] = field_v[q, part * grid : (part + 1) * grid, :].astype(BF16)
 
     def sent_theta(step, carry):
         other = lax.rem(c + step, cuts)
@@ -517,8 +507,16 @@
     def _():
         leave(t, back_ss)
 
-    for store in stores:
-        store.wait()
+
+def final_kernel(wide_ref, prop_ref, out_ref):
+    grid = prop_ref.shape[1]
+    rows, _, slots, _ = out_ref.shape
+    real_part = wide_ref[:, 0:grid]
+    imag_part = wide_ref[:, grid:]
+    out_re = dot_nt(real_part, prop_ref[0]) - dot_nt(imag_part, prop_ref[1])
+    out_ref[:, 0] = out_re.reshape(rows, slots, grid)
+    out_im = dot_nt(imag_part, prop_ref[0]) + dot_nt(real_part, prop_ref[1])
+    out_ref[:, 1] = out_im.reshape(rows, slots, grid)
 
 
 def on_device(cuts, tiles, field_in, propagator, theta, cell_x, cell_y, src_dev, src_slot, weights, coupling):
@@ -527,14 +525,27 @@
     slots, share = theta.shape
     slices = src_dev.shape[0]
     hbm = pl.BlockSpec(memory_space=pltpu.HBM)
+    vmem = pl.BlockSpec(memory_space=pltpu.VMEM)
     block = (2 * rows, grid)
     blocks = pltpu.VMEM((tiles,) + block, BF16)
     dma = pltpu.SemaphoreType.DMA
-    result = pl.pallas_call(
+    operands = (
+        theta,
+        src_dev.T,
+        src_slot.T,
+        weights.T,
+        coupling,
+        field_in.reshape(rows * 2 * slots, grid),
+        propagator,
+        cell_x,
+        cell_y,
+    )
+    operands = [pltpu.with_memory_space_constraint(value, pltpu.HBM) for value in operands]
+    wide, prop = pl.pallas_call(
         functools.partial(section_kernel, cuts, tiles),
-        out_shape=jax.ShapeDtypeStruct((rows * 2 * slots, grid), F32),
+        out_shape=[pltpu.VMEM((grid, 2 * grid), BF16), pltpu.VMEM((2, grid, grid), BF16)],
         in_specs=[hbm] * 9,
-        out_specs=hbm,
+        out_specs=[vmem, vmem],
         scratch_shapes=[
             pltpu.VMEM((slots, share), F32),
             pltpu.VMEM((2, slices), jnp.int32),
@@ -542,7 +553,6 @@
             pltpu.SMEM((2, slices), F32),
             pltpu.SMEM((2, 2), F32),
             pltpu.VMEM((grid // LANES, (rows + 1) * 2 * slots, LANES), F32),
-            pltpu.VMEM((2, grid, grid), BF16),
             pltpu.VMEM((slots, 2, share), jnp.int32),
             pltpu.VMEM((slots, 2, share), jnp.int32),
             pltpu.VMEM((16, slices), jnp.int32),
@@ -580,20 +590,16 @@
             dma((tiles,)),
         ],
         compiler_params=pltpu.CompilerParams(
-            collective_id=0, has_side_effects=True, vmem_limit_bytes=64 * 1024 * 1024
+            collective_id=0, has_side_effects=True, vmem_limit_bytes=48 * 1024 * 1024
         ),
-    )(
-        theta,
-        src_dev.T,
-        src_slot.T,
-        weights.T,
-        coupling,
-        field_in.reshape(rows * 2 * slots, grid),
-        propagator,
-        cell_x,
-        cell_y,
-    )
-    return result.reshape(rows, 2, slots, grid)
+    )(*operands)
+    return pl.pallas_call(
+        final_kernel,
+        out_shape=jax.ShapeDtypeStruct((rows, 2, slots, grid), F32),
+        in_specs=[vmem, vmem],
+        out_specs=vmem,
+        compiler_params=pltpu.CompilerParams(vmem_limit_bytes=32 * 1024 * 1024),
+    )(wide, prop)
 
 
 def solution(mesh):

time: 54 us -> 51.7 us (0.957)
  local copies, waits for them, and re-layouts: 2.36 us -> 0 us
    unnamed x1 -> x0, local copies, waits for them, and re-layouts: 2.36 us -> none
    pallas_call x0 -> x1, Pallas kernels: none -> 1.91 us  [on_device(): pl.pallas_call(final_kernel, out_shape=jax.ShapeDtypeStruct((rows, 2, slo...]
    pallas_call x1, Pallas kernels: 51.5 us -> 49.6 us  [on_device(): pl.pallas_call(functools.partial(section_kernel, cuts, tiles), out_shape=...]
where the time goes in v3:
time: 51.7 us; the launch traced here: 51.6 us
  Pallas kernels  51.5 us (100%)
    pallas_call x1, Pallas kernels, on_device(): pl.pallas_call(functools.partial(section_kernel, cuts, tiles), out_shape=...  49.6 us
    pallas_call x1, Pallas kernels, on_device(): pl.pallas_call(final_kernel, out_shape=jax.ShapeDtypeStruct((rows, 2, slo...  1.91 us

profile of v3, /device:TPU:1, one launch (start us, length us, event | category | flops | bytes accessed | tf_op | source)
XLA Modules:
  0.0 51.6 jit_solution(7595166404472558254)
XLA Ops:
  0.0 49.6 %shard_map.91 = (bf16[384,768]{1,0:T(8,128)(2,1)S(1)}, bf16[2,384,384]{2,1,0:T(8,128)(2,1)S(1)}) custom-call(f32[16,2048]{1,0:T(8,128)} %theta_hbm.1, s32[2,256]{1,0:T(2,128)} %bitcast.5, s32[2,256]{1,0:T(2,128)} %bitcast.6, f32[2,256]{1,0:T(2,128)} %bitcast.7, f32[2,2]{1,0:T(2,128)} %coupling_hbm.1, f32[768,384]{1,0:T(8,128)} %bitcast.4, ...), custom_call_target="tpu_custom_call" | custom-call | tf_op jit(solution)/shard_map/pallas_call | solution.py:544
  49.6 1.9 %shard_map.92 = f32[24,2,16,384]{3,2,1,0:T(8,128)} custom-call(bf16[384,768]{1,0:T(8,128)(2,1)S(1)} %get-tuple-element.7.wide_ref, bf16[2,384,384]{2,1,0:T(8,128)(2,1)S(1)} %get-tuple-element.8.prop_ref), custom_call_target="tpu_custom_call" | custom-call | tf_op jit(solution)/shard_map/pallas_call | solution.py:596

commit v4 on v3

--- a/solution.py
+++ b/solution.py
@@ -356,7 +356,7 @@
         def _():
             deliver(source_send.at[slot], near_recv, slot, near_ss, near_rs)
 
-        @pl.when(step == 4)
+        @pl.when(step == 12)
         def _():
             hop_copy(1, source_send.at[0], source_hop.at[0]).wait_recv()
             deliver(source_hop.at[0], far_recv, 0, far_ss, far_rs)

time: 51.7 us -> 50.3 us (0.973)
  Pallas kernels: 51.5 us -> 50.2 us
    pallas_call x1, Pallas kernels: 49.6 us -> 48.2 us  [on_device(): pl.pallas_call(functools.partial(section_kernel, cuts, tiles), out_shape=...]
where the time goes in v4:
time: 50.3 us; the launch traced here: 50.2 us
  Pallas kernels  50.2 us (100%)
    pallas_call x1, Pallas kernels, on_device(): pl.pallas_call(functools.partial(section_kernel, cuts, tiles), out_shape=...  48.2 us
    pallas_call x1, Pallas kernels, on_device(): pl.pallas_call(final_kernel, out_shape=jax.ShapeDtypeStruct((rows, 2, slo...  1.91 us

profile of v4, /device:TPU:1, one launch (start us, length us, event | category | flops | bytes accessed | tf_op | source)
XLA Modules:
  0.0 50.2 jit_solution(3356150787227210625)
XLA Ops:
  0.0 48.2 %shard_map.91 = (bf16[384,768]{1,0:T(8,128)(2,1)S(1)}, bf16[2,384,384]{2,1,0:T(8,128)(2,1)S(1)}) custom-call(f32[16,2048]{1,0:T(8,128)} %theta_hbm.1, s32[2,256]{1,0:T(2,128)} %bitcast.5, s32[2,256]{1,0:T(2,128)} %bitcast.6, f32[2,256]{1,0:T(2,128)} %bitcast.7, f32[2,2]{1,0:T(2,128)} %coupling_hbm.1, f32[768,384]{1,0:T(8,128)} %bitcast.4, ...), custom_call_target="tpu_custom_call" | custom-call | tf_op jit(solution)/shard_map/pallas_call | solution.py:544
  48.2 1.9 %shard_map.92 = f32[24,2,16,384]{3,2,1,0:T(8,128)} custom-call(bf16[384,768]{1,0:T(8,128)(2,1)S(1)} %get-tuple-element.7.wide_ref, bf16[2,384,384]{2,1,0:T(8,128)(2,1)S(1)} %get-tuple-element.8.prop_ref), custom_call_target="tpu_custom_call" | custom-call | tf_op jit(solution)/shard_map/pallas_call | solution.py:596

commit v5 on v4

--- a/solution.py
+++ b/solution.py
@@ -449,6 +449,40 @@
 
     lax.fori_loop(0, groups, chunk_out, 0)
 
+    def sent_theta(step, carry):
+        other = lax.rem(c + step, cuts)
+        theta_copy(other, other, other).wait_send()
+        return carry
+
+    lax.fori_loop(1, cuts, sent_theta, 0)
+
+    def leave(to, send):
+        block_copy(back_send.at[0], back_recv.at[0], to, send.at[to], back_rs.at[0]).wait_send()
+
+    def sent(step, carry):
+        other = lax.rem(t + step, tiles)
+        leave(other, field_ss)
+        leave(other, far_ss)
+
+        @pl.when(lax.rem(other, 2) == 1)
+        def _():
+            leave(other, near_ss)
+
+        return carry
+
+    lax.fori_loop(1, tiles, sent, 0)
+
+    @pl.when(odd)
+    def _():
+        def sent_twin(other, carry):
+            leave(other, twin_ss)
+            return carry
+
+        lax.fori_loop(0, tiles, sent_twin, 0)
+
+    hop_copy(0, field_send.at[0], field_hop.at[0]).wait_send()
+    hop_copy(1, source_send.at[0], source_hop.at[0]).wait_send()
+
     def gather(step, carry):
         group = lax.rem(t // 4 + turn(step, groups), groups)
         for i in range(4):
@@ -468,55 +502,37 @@
             at = part * grid + q * LANES
             wide_ref[:, at : at + LANES] = field_v[q, part * grid : (part + 1) * grid, :].astype(BF16)
 
-    def sent_theta(step, carry):
-        other = lax.rem(c + step, cuts)
-        theta_copy(other, other, other).wait_send()
-        return carry
-
-    lax.fori_loop(1, cuts, sent_theta, 0)
-
-    def leave(to, send):
-        block_copy(back_send.at[0], back_recv.at[0], to, send.at[to], back_rs.at[0]).wait_send()
-
-    def sent(step, carry):
-        other = lax.rem(t + step, tiles)
-        leave(other, field_ss)
-        leave(other, far_ss)
-        leave(other, back_ss)
-
-        @pl.when(lax.rem(other, 2) == 1)
-        def _():
-            leave(other, near_ss)
-
-        return carry
-
-    lax.fori_loop(1, tiles, sent, 0)
-
-    @pl.when(odd)
-    def _():
-        def sent_twin(other, carry):
-            leave(other, twin_ss)
-            return carry
-
-        lax.fori_loop(0, tiles, sent_twin, 0)
-
-    hop_copy(0, field_send.at[0], field_hop.at[0]).wait_send()
-    hop_copy(1, source_send.at[0], source_hop.at[0]).wait_send()
+    def sent_back(step, carry):
+        leave(lax.rem(t + step, tiles), back_ss)
+        return carry
+
+    lax.fori_loop(1, tiles, sent_back, 0)
 
     @pl.when(t == tiles - 1)
     def _():
         leave(t, back_ss)
 
 
-def final_kernel(wide_ref, prop_ref, out_ref):
+def final_kernel(wide_ref, prop_ref, out_hbm, whole, sems):
     grid = prop_ref.shape[1]
-    rows, _, slots, _ = out_ref.shape
-    real_part = wide_ref[:, 0:grid]
-    imag_part = wide_ref[:, grid:]
-    out_re = dot_nt(real_part, prop_ref[0]) - dot_nt(imag_part, prop_ref[1])
-    out_ref[:, 0] = out_re.reshape(rows, slots, grid)
-    out_im = dot_nt(imag_part, prop_ref[0]) + dot_nt(real_part, prop_ref[1])
-    out_ref[:, 1] = out_im.reshape(rows, slots, grid)
+    rows, _, slots, _ = whole.shape
+    rows = rows // 2
+    stores = []
+    for i in range(2):
+        real_part = wide_ref[i * rows * slots : (i + 1) * rows * slots, 0:grid]
+        imag_part = wide_ref[i * rows * slots : (i + 1) * rows * slots, grid:]
+        here = slice(i * rows, (i + 1) * rows)
+        out_re = dot_nt(real_part, prop_ref[0]) - dot_nt(imag_part, prop_ref[1])
+        whole[here, 0] = out_re.reshape(rows, slots, grid)
+        out_im = dot_nt(imag_part, prop_ref[0]) + dot_nt(real_part, prop_ref[1])
+        whole[here, 1] = out_im.reshape(rows, slots, grid)
+        store = pltpu.make_async_copy(
+            whole.at[pl.ds(i * rows, rows)], out_hbm.at[pl.ds(i * rows, rows)], sems.at[i]
+        )
+        store.start()
+        stores.append(store)
+    for store in stores:
+        store.wait()
 
 
 def on_device(cuts, tiles, field_in, propagator, theta, cell_x, cell_y, src_dev, src_slot, weights, coupling):
@@ -597,7 +613,8 @@
         final_kernel,
         out_shape=jax.ShapeDtypeStruct((rows, 2, slots, grid), F32),
         in_specs=[vmem, vmem],
-        out_specs=vmem,
+        out_specs=hbm,
+        scratch_shapes=[pltpu.VMEM((rows, 2, slots, grid), F32), dma((2,))],
         compiler_params=pltpu.CompilerParams(vmem_limit_bytes=32 * 1024 * 1024),
     )(wide, prop)
 

time: 50.3 us -> 49.8 us (0.990)
  no operation moved by 1% of the time
where the time goes in v5:
time: 49.8 us; the launch traced here: 49.7 us
  Pallas kernels  49.7 us (100%)
    pallas_call x1, Pallas kernels, on_device(): pl.pallas_call(functools.partial(section_kernel, cuts, tiles), out_shape=...  47.9 us
    pallas_call x1, Pallas kernels, on_device(): pl.pallas_call(final_kernel, out_shape=jax.ShapeDtypeStruct((rows, 2, slo...  1.84 us

profile of v5, /device:TPU:1, one launch (start us, length us, event | category | flops | bytes accessed | tf_op | source)
XLA Modules:
  0.0 49.7 jit_solution(3231092127635438382)
XLA Ops:
  0.0 47.9 %shard_map.91 = (bf16[384,768]{1,0:T(8,128)(2,1)S(1)}, bf16[2,384,384]{2,1,0:T(8,128)(2,1)S(1)}) custom-call(f32[16,2048]{1,0:T(8,128)} %theta_hbm.1, s32[2,256]{1,0:T(2,128)} %bitcast.5, s32[2,256]{1,0:T(2,128)} %bitcast.6, f32[2,256]{1,0:T(2,128)} %bitcast.7, f32[2,2]{1,0:T(2,128)} %coupling_hbm.1, f32[768,384]{1,0:T(8,128)} %bitcast.4, ...), custom_call_target="tpu_custom_call" | custom-call | tf_op jit(solution)/shard_map/pallas_call | solution.py:560
  47.9 1.8 %shard_map.92 = f32[24,2,16,384]{3,2,1,0:T(8,128)} custom-call(bf16[384,768]{1,0:T(8,128)(2,1)S(1)} %get-tuple-element.7.wide_ref, bf16[2,384,384]{2,1,0:T(8,128)(2,1)S(1)} %get-tuple-element.8.prop_ref), custom_call_target="tpu_custom_call" | custom-call | tf_op jit(solution)/shard_map/pallas_call | solution.py:612

commit v6 on v5

--- a/solution.py
+++ b/solution.py
@@ -10,6 +10,7 @@
 
 HARM = 5
 CAP = 4
+NEAR_LAG = 5
 LANES = 128
 MESH = pl.DeviceIdType.MESH
 SIN_PI = (
@@ -344,6 +345,15 @@
     hop_copy(1, source_send.at[slots - 1], source_hop.at[0]).start()
     deliver(source_send.at[slots - 1], near_recv, slots - 1, near_ss, near_rs)
 
+    def near_out(step, carry):
+        slot = lax.rem(t + turn(step, slots), slots)
+
+        @pl.when((lax.rem(slot, 2) == 1) & (slot < slots - 1))
+        def _():
+            deliver(source_send.at[slot], near_recv, slot, near_ss, near_rs)
+
+        return carry
+
     def one_slot(step, carry):
         slot = lax.rem(t + turn(step, slots), slots)
 
@@ -352,9 +362,9 @@
             deposit(slot)
             deliver(source_send.at[slot], far_recv, slot + 1, far_ss, far_rs)
 
-        @pl.when((lax.rem(slot, 2) == 1) & (slot < slots - 1))
-        def _():
-            deliver(source_send.at[slot], near_recv, slot, near_ss, near_rs)
+        @pl.when(step >= NEAR_LAG)
+        def _():
+            near_out(step - NEAR_LAG, 0)
 
         @pl.when(step == 12)
         def _():
@@ -364,6 +374,7 @@
         return carry
 
     lax.fori_loop(0, slots, one_slot, 0)
+    lax.fori_loop(slots - NEAR_LAG, slots, near_out, 0)
 
     def field_in(other, carry):
         arrive(field_recv, other, field_rs)

time: 49.8 us -> 49.5 us (level)
  no operation moved by 1% of the time
where the time goes in v6:
time: 49.5 us; the launch traced here: 49.4 us
  Pallas kernels  49.4 us (100%)
    pallas_call x1, Pallas kernels, on_device(): pl.pallas_call(functools.partial(section_kernel, cuts, tiles), out_shape=...  47.5 us
    pallas_call x1, Pallas kernels, on_device(): pl.pallas_call(final_kernel, out_shape=jax.ShapeDtypeStruct((rows, 2, slo...  1.85 us

profile of v6, /device:TPU:1, one launch (start us, length us, event | category | flops | bytes accessed | tf_op | source)
XLA Modules:
  0.0 49.4 jit_solution(8615683535455138484)
XLA Ops:
  0.0 47.5 %shard_map.91 = (bf16[384,768]{1,0:T(8,128)(2,1)S(1)}, bf16[2,384,384]{2,1,0:T(8,128)(2,1)S(1)}) custom-call(f32[16,2048]{1,0:T(8,128)} %theta_hbm.1, s32[2,256]{1,0:T(2,128)} %bitcast.5, s32[2,256]{1,0:T(2,128)} %bitcast.6, f32[2,256]{1,0:T(2,128)} %bitcast.7, f32[2,2]{1,0:T(2,128)} %coupling_hbm.1, f32[768,384]{1,0:T(8,128)} %bitcast.4, ...), custom_call_target="tpu_custom_call" | custom-call | tf_op jit(solution)/shard_map/pallas_call | solution.py:571
  47.5 1.8 %shard_map.92 = f32[24,2,16,384]{3,2,1,0:T(8,128)} custom-call(bf16[384,768]{1,0:T(8,128)(2,1)S(1)} %get-tuple-element.7.wide_ref, bf16[2,384,384]{2,1,0:T(8,128)(2,1)S(1)} %get-tuple-element.8.prop_ref), custom_call_target="tpu_custom_call" | custom-call | tf_op jit(solution)/shard_map/pallas_call | solution.py:623
